TPU v7x, 256 devices: a whole 4x4x8 slice. The times are simulated.
256 devices in a mesh: rep: 8 (over y, z_lo), fsdp: 32 (over x, z_hi, core).
Axes of the slice: x: 4, y: 4, z: 8 (z_hi: 4, z_lo: 2; z = z_hi * 2 + z_lo), core: 2. Of those that a mesh axis runs over, the one named last changes fastest.
Arguments:
- token_ids: int32 [8, 8192], P('rep', 'fsdp'), may hold values from 0 to 255
- targets: int32 [8, 8192], P('rep', 'fsdp'), may hold values from 0 to 255
- fragment: int32 [12288], P('fsdp'), may hold values from 0 to 1
- inner_weights: float32 [8, 2, 12288, 256], P('rep', None, 'fsdp'), may hold values from -12 to 12
- first_moment: float32 [8, 2, 12288, 256], P('rep', None, 'fsdp'), may hold values from -6 to 6
- second_moment: float32 [8, 2, 12288, 256], P('rep', None, 'fsdp'), may hold values from 0.25 to 4
- outer_base: float32 [12288, 256], P('fsdp'), may hold values from -6 to 6
- outer_momentum: float32 [12288, 256], P('fsdp'), may hold values from -4 to 4
Outputs:
- new_weights: float32 [8, 2, 12288, 256], P('rep', None, 'fsdp')
- new_first: float32 [8, 2, 12288, 256], P('rep', None, 'fsdp')
- new_second: float32 [8, 2, 12288, 256], P('rep', None, 'fsdp')
- new_base: float32 [12288, 256], P('fsdp')
- new_momentum: float32 [12288, 256], P('fsdp')
All inputs are finite; a program needn't handle non-finite values.
Results may differ from a plain program's by a relative error of at most 0.04.
Values may be sent and summed in bfloat16 or wider, within the bound.
A program may use at most 128 MiB of HBM per device.

v0:
```python
import math

import jax
import jax.numpy as jnp
from jax import lax
from jax.sharding import PartitionSpec as P

D = 12288
VOCAB = 256


def shards(
    token_ids,
    targets,
    fragment,
    inner_weights,
    first_moment,
    second_moment,
    outer_base,
    outer_momentum,
):
    tok_ids = token_ids[0]
    labels = targets[0]
    weights = inner_weights[0]
    table_local = weights[0].astype(jnp.bfloat16)
    head_local = weights[1].astype(jnp.bfloat16)
    logit_scale = 3.0 / math.sqrt(D)
    vocab_iota = jnp.arange(VOCAB, dtype=jnp.int32)
    target_hot = (labels[:, None] == vocab_iota[None, :]).astype(jnp.float32)
    own_tokens = tok_ids.shape[0]
    grad_scale = math.sqrt(VOCAB / own_tokens)
    embedded = jnp.take(lax.all_gather(table_local, "fsdp", axis=0, tiled=True).T, tok_ids, axis=0)
    widened = embedded.astype(jnp.float32)
    inv_rms = lax.rsqrt(jnp.mean(widened * widened, axis=-1, keepdims=True) + 1e-05)
    unit_rows = widened * inv_rms
    normed = unit_rows.astype(jnp.bfloat16)
    head_full = lax.all_gather(head_local, "fsdp", axis=0, tiled=True)
    logits = jnp.dot(normed, head_full, preferred_element_type=jnp.float32) * logit_scale
    probabilities = jax.nn.softmax(logits, axis=-1)
    logit_grad = (grad_scale * (probabilities - target_hot)).astype(jnp.bfloat16)
    columns = normed
    head_grad = lax.psum_scatter(
        lax.dot_general(
            columns, logit_grad, (((0,), (0,)), ((), ())), preferred_element_type=jnp.float32
        ).astype(jnp.bfloat16),
        "fsdp",
        scatter_dimension=0,
        tiled=True,
    ).astype(jnp.float32)
    normed_grad = lax.dot_general(
        logit_grad, head_full, (((1,), (1,)), ((), ())), preferred_element_type=jnp.float32
    )
    embed_grad = (
        inv_rms
        * (normed_grad - unit_rows * jnp.mean(normed_grad * unit_rows, axis=-1, keepdims=True))
    ).astype(jnp.bfloat16)
    id_hot = (tok_ids[:, None] == vocab_iota[None, :]).astype(jnp.bfloat16)
    columns = embed_grad
    table_grad = lax.psum_scatter(
        lax.dot_general(
            columns, id_hot, (((0,), (0,)), ((), ())), preferred_element_type=jnp.float32
        ).astype(jnp.bfloat16),
        "fsdp",
        scatter_dimension=0,
        tiled=True,
    ).astype(jnp.float32)
    gradients = jnp.stack([table_grad, head_grad])
    new_first = 0.9 * first_moment[0] + 0.1 * gradients
    new_second = 0.95 * second_moment[0] + 0.05 * gradients * gradients
    stepped = weights - 0.05 * (new_first / (jnp.sqrt(new_second) + 1e-08) + 0.1 * weights)
    chosen = jnp.where((fragment == 1)[:, None], weights[1], weights[0])
    difference = outer_base - chosen
    replica_count = lax.axis_size("rep")
    outer_delta = (
        lax.psum(difference.astype(jnp.bfloat16), "rep").astype(jnp.float32) / replica_count
    )
    new_momentum = 0.9 * outer_momentum + outer_delta
    new_base = outer_base - 0.7 * (outer_delta + 0.9 * new_momentum)
    is_fragment = (jnp.arange(2, dtype=jnp.int32)[:, None] == fragment[None, :])[:, :, None]
    new_weights = jnp.where(is_fragment, 0.5 * stepped + 0.5 * new_base[None], stepped)
    return (new_weights[None], new_first[None], new_second[None], new_base, new_momentum)


def solution(mesh):
    in_specs = (
        P("rep", "fsdp"),
        P("rep", "fsdp"),
        P("fsdp"),
        P("rep", None, "fsdp", None),
        P("rep", None, "fsdp", None),
        P("rep", None, "fsdp", None),
        P("fsdp", None),
        P("fsdp", None),
    )
    out_specs = (
        P("rep", None, "fsdp", None),
        P("rep", None, "fsdp", None),
        P("rep", None, "fsdp", None),
        P("fsdp", None),
        P("fsdp", None),
    )
    return jax.shard_map(shards, mesh=mesh, in_specs=in_specs, out_specs=out_specs, check_vma=False)
```

profile of v0, /device:TPU:8, one launch (start us, length us, event | category | flops | bytes accessed | tf_op | source)
XLA Modules:
  0.0 425.6 jit_solution(12286111197540193832)
XLA Ops:
  8.0 0.0 all-gather.3.cloned.1.call-start
  8.1 1.2 fusion.26
  9.2 0.2 copy.29
  9.4 0.7 bitcast_convert_fusion.1
  10.1 0.0 all-gather.5.cloned.1.call-start
  10.2 0.2 copy.30
  10.3 0.7 bitcast_convert_fusion
  11.1 0.0 all-reduce.2.cloned.1.call-start
  11.1 1.2 copy.25
  12.3 0.7 broadcast_compare_fusion
  13.0 0.7 fusion.20
  13.7 0.0 reduce-scatter.3.cloned.1.call-start
  13.8 76.6 %all-gather.3.cloned.1.call-done = bf16[12288,256]{0,1:T(8,128)(2,1)} async-done(((bf16[384,256]{0,1:T(8,128)(2,1)}), bf16[12288,256]{0,1:T(8,128)(2,1)}) %all-gather.3.cloned.1.call-update) | async-done | bytes 6291472 | tf_op jit(solution)/shard_map/all_gather | solution.py:32
  90.4 16.3 %gather_fusion = bf16[256,12288]{1,0:T(8,128)(2,1)} fusion(bf16[256,12288]{1,0:T(8,128)(2,1)} %bitcast.20, s32[1024]{0:T(1024)S(1)} %pad_clamp_fusion), kind=kCustom, calls=%fused_computation | custom fusion | bytes 12583936 | tf_op jit(solution)/shard_map/jit(_take)/gather | solution.py:32
  106.7 4.8 %fusion.7 = f32[256]{0:T(256)S(1)} fusion(bf16[256,12288]{1,0:T(8,128)(2,1)} %gather_fusion, pred[256]{0:T(512)(128)(4,1)S(1)} %compare_and_fusion), kind=kLoop, calls=%fused_computation.12 | loop fusion | flops 12582656 | bytes 6292736 | tf_op jit(solution)/shard_map/reduce_sum | solution.py:34
  111.5 56.2 %all-gather.5.cloned.1.call-done = bf16[12288,256]{0,1:T(8,128)(2,1)} async-done(((bf16[384,256]{0,1:T(8,128)(2,1)}), bf16[12288,256]{0,1:T(8,128)(2,1)}) %all-gather.5.cloned.1.call-update) | async-done | bytes 6291472 | tf_op jit(solution)/shard_map/all_gather | solution.py:37
  167.7 7.1 %fusion.27 = (f32[256]{0:T(256)S(1)}, f32[256,256]{0,1:T(8,128)S(1)}) fusion(bf16[12288,256]{0,1:T(8,128)(2,1)} %all-gather.5.cloned.1.call-done, f32[256]{0:T(256)S(1)} %add_rsqrt_fusion, bf16[256,12288]{1,0:T(8,128)(2,1)} %gather_fusion, pred[256]{0:T(512)(128)(4,1)S(1)} %compare_and_fusion), kind=kOutput, calls=%fused_computation.49 | convolution fusion | flops 1623326464 | bytes 12847360 | tf_op jit(solution)/shard_map/dot_general | solution.py:38
  174.8 0.1 fusion.21
  174.9 9.1 %fusion.3 = (f32[256]{0:T(256)S(1)}, f32[256,12288]{1,0:T(8,128)}) fusion(f32[256]{0:T(256)S(1)} %add_rsqrt_fusion, bf16[256,12288]{1,0:T(8,128)(2,1)} %gather_fusion, pred[256]{0:T(512)(128)(4,1)S(1)} %compare_and_fusion, bf16[12288,256]{0,1:T(8,128)(2,1)S(1)} %copy-done, f32[256,256]{0,1:T(8,128)S(1)} %get-tuple-element.24, s32[256]{0:T(256)S(1)} %bitcast.25, ...), kind=kOutput, calls=%fused_computation.8 | convolution fusion | flops 1626734336 | bytes 25433344 | tf_op jit(solution)/shard_map/dot_general | solution.py:50
  184.0 11.7 %convolution_convert_fusion.1 = bf16[12288,256]{1,0:T(8,128)(2,1)} fusion(f32[256,12288]{1,0:T(8,128)} %get-tuple-element.26, f32[256]{0:T(256)S(1)} %broadcast_multiply_fusion.1, f32[256]{0:T(256)S(1)} %add_rsqrt_fusion, s32[256]{0:T(256)S(1)} %bitcast.29, bf16[256,12288]{1,0:T(8,128)(2,1)S(1)} %bitcast.22, pred[256]{0:T(512)(128)(4,1)S(1)} %compare_and_fusion), kind=kOutput, calls=%fused_computation.7 | convolution fusion | flops 1635844096 | bytes 25169152 | tf_op jit(solution)/shard_map/dot_general | solution.py:60
  195.7 0.3 reduce-scatter.5.cloned.1.call-start
  196.0 7.6 %convolution_convert_fusion = bf16[12288,256]{1,0:T(8,128)(2,1)} fusion(f32[256]{0:T(256)S(1)} %add_rsqrt_fusion, f32[256,256]{0,1:T(8,128)S(1)} %get-tuple-element.24, s32[256]{0:T(256)S(1)} %bitcast.26, f32[256]{0:T(256)S(1)} %fusion.21, f32[256]{0:T(256)S(1)} %get-tuple-element.23, bf16[256,12288]{1,0:T(8,128)(2,1)} %gather_fusion, ...), kind=kOutput, calls=%fused_computation.6 | convolution fusion | flops 1626734592 | bytes 12849408 | tf_op jit(solution)/shard_map/dot_general | solution.py:43
  203.6 1.0 copy-done.3
  204.6 0.2 copy.24
  204.8 0.0 all-reduce.2.cloned.1.call-done
  204.8 1.1 broadcast_multiply_fusion
  205.9 0.2 copy.26
  206.0 0.9 copy.27
  206.9 0.9 copy.28
  207.9 96.3 %reduce-scatter.3.cloned.1.call-done = bf16[384,256]{1,0:T(8,128)(2,1)} async-done(((bf16[12288,256]{1,0:T(8,128)(2,1)}), bf16[384,256]{1,0:T(8,128)(2,1)}) %reduce-scatter.3.cloned.1.call-update) | async-done | bytes 196624 | tf_op jit(solution)/shard_map/reduce_scatter | solution.py:59
  304.1 111.0 %reduce-scatter.5.cloned.1.call-done = bf16[384,256]{1,0:T(8,128)(2,1)} async-done(((bf16[12288,256]{1,0:T(8,128)(2,1)}), bf16[384,256]{1,0:T(8,128)(2,1)}) %reduce-scatter.5.cloned.1.call-update) | async-done | bytes 196624 | tf_op jit(solution)/shard_map/reduce_scatter | solution.py:42
  415.1 3.4 add_select_fusion
  (29 shorter events, 0.2 us)
Async XLA Ops:
  8.0 5.8 %copy-start.6 = (s32[1,256]{1,0:T(1,128)S(1)}, s32[1,256]{1,0:T(1,128)}, u32[]{:S(2)}) copy-start(s32[1,256]{1,0:T(1,128)} %param.8) | copy-start | bytes 3076
  8.0 82.4 %all-gather.3.cloned.1.call-start = ((), (), s32[]{:S(2)}) async-start(), calls=%async_computation.2 | async-start | bytes 6488064 | tf_op jit(solution)/shard_map/all_gather | solution.py:32
  10.1 157.6 %all-gather.5.cloned.1.call-start = ((), (), s32[]{:S(2)}) async-start(), calls=%async_computation.3 | async-start | bytes 6488064 | tf_op jit(solution)/shard_map/all_gather | solution.py:37
  11.1 193.7 %all-reduce.2.cloned.1.call-start = ((), (), s32[]{:S(2)}) async-start(), calls=%async_computation.6 | async-start | bytes 393216 | tf_op jit(solution)/shard_map/psum | solution.py:75
  13.7 290.4 %reduce-scatter.3.cloned.1.call-start = ((), (), s32[]{:S(2)}) async-start(), calls=%async_computation.4 | async-start | bytes 6488064 | tf_op jit(solution)/shard_map/reduce_scatter | solution.py:59
  111.5 63.5 %copy-start.5 = (s32[1,256]{1,0:T(1,128)S(1)}, s32[1,256]{1,0:T(1,128)}, u32[]{:S(2)}) copy-start(s32[1,256]{1,0:T(1,128)} %param.9) | copy-start | bytes 3076
  167.7 7.2 %copy-start = (bf16[12288,256]{0,1:T(8,128)(2,1)S(1)}, bf16[12288,256]{0,1:T(8,128)(2,1)}, u32[]{:S(2)}) copy-start(bf16[12288,256]{0,1:T(8,128)(2,1)} %all-gather.5.cloned.1.call-done) | copy-start | bytes 18874372
  167.7 16.3 %slice-start = ((s8[6291456]{0:T(1024)(128)(4,1)}), s8[4194304]{0:T(1024)(128)(4,1)S(1)}, s32[]{:S(2)}) async-start(s8[6291456]{0:T(1024)(128)(4,1)} %bitcast.21), calls=%async_computation.7 | async-start | bytes 8388608
  174.9 9.1 %slice-start.1 = ((s8[6291456]{0:T(1024)(128)(4,1)}), s8[2097152]{0:T(1024)(128)(4,1)S(1)}, s32[]{:S(2)}) async-start(s8[6291456]{0:T(1024)(128)(4,1)} %bitcast.21), calls=%async_computation.8 | async-start | bytes 4194304
  195.7 219.4 %reduce-scatter.5.cloned.1.call-start = ((), (), s32[]{:S(2)}) async-start(), calls=%async_computation.5 | async-start | bytes 6488064 | tf_op jit(solution)/shard_map/reduce_scatter | solution.py:42
  203.6 1.0 copy-start.3
  203.6 1.2 copy-start.4
  203.6 211.5 %copy-start.1 = (f32[1,2,384,256]{3,2,1,0:T(8,128)S(1)}, f32[1,2,384,256]{3,2,1,0:T(8,128)}, u32[]{:S(2)}) copy-start(f32[1,2,384,256]{3,2,1,0:T(8,128)} %param.11) | copy-start | bytes 2359300
  203.6 211.5 %copy-start.2 = (f32[1,2,384,256]{3,2,1,0:T(8,128)S(1)}, f32[1,2,384,256]{3,2,1,0:T(8,128)}, u32[]{:S(2)}) copy-start(f32[1,2,384,256]{3,2,1,0:T(8,128)} %param.13) | copy-start | bytes 2359300
Sparse Core Ops, SparseCore 0:
  12.2 78.1 all-gather.2
  93.7 73.9 all-gather.4
  195.8 108.2 reduce-scatter.2
  308.0 107.0 reduce-scatter.4
Sparse Core Ops, SparseCore 1:
  14.7 95.3 all-reduce.1
where the time goes:
time: 426 us
  waiting for transfers between devices  340 us (80%)
  matrix products  35.4 us (8%)
  local copies, waits for them, and re-layouts  22.1 us (5%)
  between operations  15.4 us (4%)
  other arithmetic  12.1 us (3%)
    reduce_scatter x1, waiting for transfers between devices, shards(): lax.psum_scatter(lax.dot_general(columns, logit_grad, (((0,), (0,)), ((),...  111 us
    reduce_scatter x1, waiting for transfers between devices, shards(): lax.psum_scatter(lax.dot_general(columns, id_hot, (((0,), (0,)), ((), ())...  96.3 us
    all_gather x1, waiting for transfers between devices, shards(): lax.all_gather(table_local, 'fsdp', axis=0, tiled=True)  76.6 us
    all_gather x1, waiting for transfers between devices, shards(): head_full = lax.all_gather(head_local, 'fsdp', axis=0, tiled=True)  56.2 us
    gather x1, local copies, waits for them, and re-layouts, shards(): jnp.take(lax.all_gather(table_local, 'fsdp', axis=0, tiled=True).T, tok_i...  16.3 us
    dot_general x1, matrix products, shards(): lax.dot_general(columns, id_hot, (((0,), (0,)), ((), ())), preferred_elem...  11.7 us
    dot_general x1, matrix products, shards(): lax.dot_general(logit_grad, head_full, (((1,), (1,)), ((), ())), preferre...  9.06 us
  transfers between devices with their start and end apart: 5, of which 4 were waited for; matrix products, arithmetic and copies ran while one was open for 15% of the time, Pallas kernels for 0%

commit v1 on v0

v1 whole, which is shorter than its diff:
```python
import math

import jax
import jax.numpy as jnp
from jax import lax
from jax.sharding import PartitionSpec as P

D = 12288
VOCAB = 256


def shards(
    token_ids,
    targets,
    fragment,
    inner_weights,
    first_moment,
    second_moment,
    outer_base,
    outer_momentum,
):
    weights = inner_weights[0]
    table = weights[0].astype(jnp.bfloat16)
    head = weights[1].astype(jnp.bfloat16)
    vocab_iota = jnp.arange(VOCAB, dtype=jnp.int32)
    id_hot = (token_ids[0][:, None] == vocab_iota[None, :]).astype(jnp.bfloat16)
    target_hot = (targets[0][:, None] == vocab_iota[None, :]).astype(jnp.bfloat16)

    def columns_product(a, b):
        return lax.dot_general(
            a, b, (((0,), (0,)), ((), ())), preferred_element_type=jnp.float32
        )

    wide = table.astype(jnp.float32)
    squares = jnp.sum(wide * wide, axis=0)
    sums = lax.psum(
        jnp.concatenate(
            [
                columns_product(table, head),
                columns_product(id_hot, target_hot),
                jnp.broadcast_to(squares[:, None], (VOCAB, 128)),
            ],
            axis=1,
        ),
        "fsdp",
    )
    gram, counts, squares = sums[:, :VOCAB], sums[:, VOCAB : 2 * VOCAB], sums[:, 2 * VOCAB :][:, :1]
    inv_rms = lax.rsqrt(squares / D + 1e-05)
    probabilities = jax.nn.softmax((3.0 / math.sqrt(D)) * inv_rms * gram, axis=-1)
    summed_grad = inv_rms * (jnp.sum(counts, axis=1, keepdims=True) * probabilities - counts)
    along = inv_rms * inv_rms * jnp.sum(summed_grad * gram, axis=1, keepdims=True) / D
    sent = summed_grad.astype(jnp.bfloat16)
    head_grad = jnp.dot(table, sent, preferred_element_type=jnp.float32)
    table_grad = (
        lax.dot_general(head, sent, (((1,), (1,)), ((), ())), preferred_element_type=jnp.float32)
        - wide * along[:, 0][None, :]
    )
    gradients = jnp.stack([table_grad, head_grad])
    new_first = 0.9 * first_moment[0] + 0.1 * gradients
    new_second = 0.95 * second_moment[0] + 0.05 * gradients * gradients
    stepped = weights - 0.05 * (new_first / (jnp.sqrt(new_second) + 1e-08) + 0.1 * weights)
    chosen = jnp.where((fragment == 1)[:, None], weights[1], weights[0])
    difference = outer_base - chosen
    replica_count = lax.axis_size("rep")
    outer_delta = (
        lax.psum(difference.astype(jnp.bfloat16), "rep").astype(jnp.float32) / replica_count
    )
    new_momentum = 0.9 * outer_momentum + outer_delta
    new_base = outer_base - 0.7 * (outer_delta + 0.9 * new_momentum)
    is_fragment = (jnp.arange(2, dtype=jnp.int32)[:, None] == fragment[None, :])[:, :, None]
    new_weights = jnp.where(is_fragment, 0.5 * stepped + 0.5 * new_base[None], stepped)
    return (new_weights[None], new_first[None], new_second[None], new_base, new_momentum)


def solution(mesh):
    in_specs = (
        P("rep", "fsdp"),
        P("rep", "fsdp"),
        P("fsdp"),
        P("rep", None, "fsdp", None),
        P("rep", None, "fsdp", None),
        P("rep", None, "fsdp", None),
        P("fsdp", None),
        P("fsdp", None),
    )
    out_specs = (
        P("rep", None, "fsdp", None),
        P("rep", None, "fsdp", None),
        P("rep", None, "fsdp", None),
        P("fsdp", None),
        P("fsdp", None),
    )
    return jax.shard_map(shards, mesh=mesh, in_specs=in_specs, out_specs=out_specs, check_vma=False)
```

time: 426 us -> 390 us (0.915)
  matrix products: 35.4 us -> 1.07 us
  waiting for transfers between devices: 340 us -> 352 us
  local copies, waits for them, and re-layouts: 22.1 us -> 13.1 us
    psum x0 -> x1, waiting for transfers between devices: none -> 276 us  [shards(): lax.psum(jnp.concatenate([columns_product(table, head), columns_product(i...]
    reduce_scatter x2 -> x0, waiting for transfers between devices: 207 us -> none  [the longest x1 111 us: shards(): lax.psum_scatter(lax.dot_general(columns, logit_grad, (((0,), (0,)), ((),...]
    all_gather x2 -> x0, waiting for transfers between devices: 133 us -> none  [the longest x1 76.6 us: shards(): lax.all_gather(table_local, 'fsdp', axis=0, tiled=True)]
    psum x1, waiting for transfers between devices: 0.03 us -> 75.6 us  [shards(): lax.psum(difference.astype(jnp.bfloat16), 'rep').astype(jnp.float32)]
    dot_general x4, matrix products: 35.4 us -> 1.07 us  [the longest x2 0.6 us: columns_product(): lax.dot_general(a, b, (((0,), (0,)), ((), ())), preferred_element_type=jn...]
    gather x1 -> x0, local copies, waits for them, and re-layouts: 16.3 us -> none  [shards(): jnp.take(lax.all_gather(table_local, 'fsdp', axis=0, tiled=True).T, tok_i...]
    unnamed x24 -> x28, local copies, waits for them, and re-layouts: 4.47 us -> 13.1 us
  transfers between devices with their start and end apart: 5 -> 2, of which waited for: 4 -> 2; matrix products, arithmetic and copies ran while one was open for 15% -> 2% of each run, Pallas kernels for 0% -> 0%
where the time goes in v1:
time: 390 us; the launch traced here: 389 us
  waiting for transfers between devices  352 us (90%)
  between operations  14.2 us (4%)
  local copies, waits for them, and re-layouts  13.1 us (3%)
  other arithmetic  9.08 us (2%)
    psum x1, waiting for transfers between devices, shards(): lax.psum(jnp.concatenate([columns_product(table, head), columns_product(i...  276 us
    psum x1, waiting for transfers between devices, shards(): lax.psum(difference.astype(jnp.bfloat16), 'rep').astype(jnp.float32)  75.6 us
    unnamed x28, local copies, waits for them, and re-layouts  13.1 us
  transfers between devices with their start and end apart: 2, of which 2 were waited for; matrix products, arithmetic and copies ran while one was open for 2% of the time, Pallas kernels for 0%

profile of v1, /device:TPU:8, one launch (start us, length us, event | category | flops | bytes accessed | tf_op | source)
XLA Modules:
  0.0 389.3 jit_solution(3632249335101254972)
XLA Ops:
  7.2 0.0 all-reduce.5.cloned.1.call-start
  7.2 0.8 broadcast_compare_fusion
  8.0 1.2 copy.21
  9.1 0.3 copy.18
  9.4 0.8 fusion.3
  10.2 0.0 all-reduce.3.cloned.1.call-start
  10.3 0.3 fusion.10
  10.5 0.4 copy-done.8
  10.9 0.3 copy-done.7
  11.2 0.3 fusion.6
  11.6 0.9 pad_maximum_fusion.1
  12.5 0.2 copy-done.5
  12.7 0.2 copy.20
  12.9 0.8 copy-done.4
  13.6 0.3 copy.13
  13.9 1.4 copy.16
  15.3 75.6 %all-reduce.5.cloned.1.call-done = bf16[384,256]{0,1:T(8,128)(2,1)} async-done(((bf16[384,256]{0,1:T(8,128)(2,1)}), bf16[384,256]{0,1:T(8,128)(2,1)}) %all-reduce.5.cloned.1.call-update) | async-done | bytes 196624 | tf_op jit(solution)/shard_map/psum | solution.py:66
  90.9 1.9 broadcast_multiply_fusion
  92.9 1.9 copy.25
  94.8 0.9 copy.26
  95.7 276.1 %all-reduce.3.cloned.1.call-done = f32[256,640]{0,1:T(8,128)} async-done(((f32[256,640]{0,1:T(8,128)}), f32[256,640]{0,1:T(8,128)}) %all-reduce.3.cloned.1.call-update) | async-done | bytes 655376 | tf_op jit(solution)/shard_map/psum | solution.py:36
  371.8 0.8 broadcast_multiply_fusion.1
  372.5 1.0 fusion.7
  373.5 1.1 slice_reduce_fusion
  374.7 0.1 multiply_reduce_fusion
  374.8 0.2 convolution_bitcast_fusion
  375.0 0.3 fusion.1
  375.3 0.7 copy-done.2
  376.0 1.7 add_select_fusion
  377.8 2.4 copy.22
  380.1 1.1 copy.24
  381.3 1.1 copy.23
  (18 shorter events, 0.1 us)
Async XLA Ops:
  7.2 2.0 copy-start.3
  7.2 83.8 %all-reduce.5.cloned.1.call-start = ((), (), s32[]{:S(2)}) async-start(), calls=%async_computation.1 | async-start | bytes 393216 | tf_op jit(solution)/shard_map/psum | solution.py:66
  10.2 361.6 %all-reduce.3.cloned.1.call-start = ((), (), s32[]{:S(2)}) async-start(), calls=%async_computation | async-start | bytes 1310720 | tf_op jit(solution)/shard_map/psum | solution.py:36
  10.3 0.7 copy-start.8
  10.5 0.7 copy-start.7
  11.6 1.1 copy-start.5
  12.5 1.2 copy-start.4
  13.9 1.4 copy-start.6
  371.8 2.9 copy-start.1
  375.0 1.0 copy-start.2
  377.8 2.4 copy-start
Sparse Core Ops, SparseCore 0:
  11.2 79.6 all-reduce.4
  94.3 277.3 all-reduce.2
